TPU v7x, 32 devices: a whole 2x2x4 slice. The times are simulated.
32 devices in a mesh: space: 8 (over z, y), chan: 4 (over x, core).
Axes of the slice: x: 2, y: 2, z: 4, core: 2. Of those that a mesh axis runs over, the one named last changes fastest.
Arguments:
- fine_tiles: bfloat16 [256, 96, 512], P('space', 'chan'), may hold values from -6 to 6
- parent_route: int32 [256, 1], P('space'), may hold values from 0 to 7; in each aligned block of 32 rows (0 to 31, 32 to 63, ...) at most 8 rows name the same one
- parent_slots: int32 [64, 8], P('space'), may hold values from 0 to 63, as said below
- w_down: bfloat16 [8, 96, 192], replicated, may hold values from -0.21875 to 0.21875
- coarse_bias: float32 [192], replicated, may hold values from -4 to 4
- w_mid: bfloat16 [192, 192], replicated, may hold values from -0.4375 to 0.4375
- w_up: bfloat16 [8, 192, 96], replicated, may hold values from -0.4375 to 0.4375
Outputs:
- fine_out: bfloat16 [256, 96, 512], P('space', 'chan')
Inputs may be any that keep to these rules, and one draw needn't show every extreme that they name: `parent_route`: within the rows of one device no device is named by more than 8 rows, and this bound is reached. `parent_slots`: the 64 entries of one device's coarse blocks are a permutation of 0 to 63.
All inputs are finite; a program needn't handle non-finite values.
Results may differ from a plain program's by a relative error of at most 0.013.
Values may be sent and summed in bfloat16 or wider, within the bound.
A program may use at most 64 MiB of HBM per device.

v0:
```python
import jax
import jax.numpy as jnp
from jax import lax
from jax.sharding import PartitionSpec as P


def partner_octants(values):
    shaped = values.reshape(values.shape[0], 4, 2, values.shape[2], values.shape[3])
    return shaped[:, :, ::-1].reshape(values.shape)


def local(fine_tiles, parent_route, parent_slots, w_down, coarse_bias, w_mid, w_up):
    space_count = lax.axis_size("space")
    chan_count = lax.axis_size("chan")
    chan_rank = lax.axis_index("chan")
    blocks, fine_share, voxel_count = fine_tiles.shape
    cells = voxel_count // 8
    coarse_width = w_down.shape[2]
    coarse_share = coarse_width // chan_count
    coarse_count = parent_slots.shape[0]
    slot_count = coarse_count * 8
    capacity = slot_count // space_count
    destinations = parent_route[:, 0]
    matches = (destinations[:, None] == jnp.arange(space_count, dtype=jnp.int32)[None, :]).astype(
        jnp.int32
    )
    within_rank = jnp.sum(matches * (jnp.cumsum(matches, axis=0) - 1), axis=1)
    send_slot = destinations * capacity + within_rank
    parent_flat = parent_slots.reshape(-1)
    own_rows = lax.dynamic_slice_in_dim(w_down, chan_rank * fine_share, fine_share, 1)
    outgoing = (
        jnp.zeros((slot_count, fine_share, voxel_count), jnp.bfloat16).at[send_slot].set(fine_tiles)
    )
    outgoing = outgoing.reshape(space_count, capacity, fine_share, voxel_count)
    arrived = lax.all_to_all(outgoing, "space", split_axis=0, concat_axis=0, tiled=True)
    shaped = arrived.reshape(arrived.shape[0], arrived.shape[1], fine_share, 8, cells)
    partial_sums = jnp.einsum(
        "skiop,oic->skcp", shaped, own_rows, preferred_element_type=jnp.float32
    )
    arranged = partial_sums.reshape(slot_count, coarse_width, cells)[parent_flat]
    arranged = arranged.reshape(coarse_count, 8, coarse_width, cells)
    coarse_pre = lax.psum_scatter(arranged, "chan", scatter_dimension=2, tiled=True).astype(
        jnp.bfloat16
    )
    bias_share = lax.dynamic_slice_in_dim(coarse_bias, chan_rank * coarse_share, coarse_share, 0)
    coarse_act = jax.nn.silu(
        coarse_pre.astype(jnp.float32) + bias_share[None, None, :, None]
    ).astype(jnp.bfloat16)
    own_mid = lax.dynamic_slice_in_dim(w_mid, chan_rank * coarse_share, coarse_share, 1)
    incoming = lax.all_gather(coarse_act, "chan", axis=2, tiled=True)
    weights = own_mid
    direct = jnp.einsum("gqcp,ce->gqep", incoming, weights, preferred_element_type=jnp.float32)
    partner = jnp.einsum(
        "gqcp,ce->gqep", partner_octants(incoming), weights, preferred_element_type=jnp.float32
    )
    coarse_out = (direct + partner).astype(jnp.bfloat16)
    going_back = (
        jnp.zeros((slot_count, coarse_share * cells), jnp.bfloat16)
        .at[parent_flat]
        .set(coarse_out.reshape(slot_count, coarse_share * cells))
    )
    returned = lax.all_to_all(
        going_back.reshape(space_count, capacity, coarse_share * cells),
        "space",
        split_axis=0,
        concat_axis=0,
        tiled=True,
    )
    own_octants = returned.reshape(slot_count, coarse_share, cells)[send_slot]
    own_up = lax.dynamic_slice_in_dim(w_up, chan_rank * fine_share, fine_share, 2)
    weights = own_up
    lifted = jnp.einsum(
        "jcp,ocf->jfop",
        lax.all_gather(own_octants, "chan", axis=1, tiled=True),
        weights,
        preferred_element_type=jnp.float32,
    )
    return (
        fine_tiles.astype(jnp.float32) + lifted.reshape(blocks, fine_share, voxel_count)
    ).astype(jnp.bfloat16)


def solution(mesh):
    in_specs = (P("space", "chan", None), P("space", None), P("space", None), P(), P(), P(), P())
    out_specs = P("space", "chan", None)
    return jax.shard_map(local, mesh=mesh, in_specs=in_specs, out_specs=out_specs, check_vma=False)
```

profile of v0, /device:TPU:1, one launch (start us, length us, event | category | flops | bytes accessed | tf_op | source)
XLA Modules:
  0.0 220.2 jit_solution(4100064542187186932)
XLA Ops:
  6.5 0.8 fusion.15
  7.4 0.8 select_reduce_fusion
  8.9 1.3 broadcast_in_dim.5
  10.2 4.5 %scatter_fusion = bf16[64,24,512]{2,1,0:T(8,128)(2,1)} fusion(bf16[64,24,512]{2,1,0:T(8,128)(2,1)} %broadcast_in_dim.5, s32[32]{0:T(128)S(1)} %fusion.21, bf16[32,24,512]{2,1,0:T(8,128)(2,1)S(1)} %copy-done.3), kind=kCustom, calls=%fused_computation.2 | custom fusion | bytes 2359424 | tf_op jit(solution)/shard_map/scatter | solution.py:32
  14.7 6.6 %all-to-all-start = ((bf16[8,8,24,512]{3,2,1,0:T(8,128)(2,1)}), bf16[8,8,24,512]{3,2,1,0:T(8,128)(2,1)}, u32[]{:S(2)}, u32[]{:S(2)}) async-start(bf16[8,8,24,512]{3,2,1,0:T(8,128)(2,1)} %bitcast.3), calls=%async_computation | async-start | bytes 3145728 | tf_op jit(solution)/shard_map/all_to_all | solution.py:35
  21.4 36.1 %all-to-all-done = bf16[8,8,24,512]{3,2,1,0:T(8,128)(2,1)} async-done(((bf16[8,8,24,512]{3,2,1,0:T(8,128)(2,1)}), bf16[8,8,24,512]{3,2,1,0:T(8,128)(2,1)}, u32[]{:S(2)}, u32[]{:S(2)}) %all-to-all-start) | async-done | bytes 1572896 | tf_op jit(solution)/shard_map/all_to_all | solution.py:35
  57.4 3.9 %reshape.65 = bf16[8,8,24,8,64]{4,3,2,1,0:T(8,128)(2,1)S(1)} reshape(bf16[8,8,24,512]{3,2,1,0:T(8,128)(2,1)} %all-to-all-done) | data formatting | bytes 3145728 | tf_op jit(solution)/shard_map/reshape | solution.py:36
  61.4 3.2 %fusion = f32[192,8,8,64,1]{0,3,4,2,1:T(8,128)} fusion(bf16[8,8,24,8,64]{4,3,2,1,0:T(8,128)(2,1)S(1)} %reshape.65, bf16[8,96,192]{2,1,0:T(8,128)(2,1)S(1)} %copy-done, s32[]{:T(128)S(6)} %select_n.24), kind=kOutput, calls=%fused_computation.4 | convolution fusion | flops 301989888 | bytes 6389764 | tf_op jit(solution)/shard_map/skiop,oic->skcp/dot_general | solution.py:37
  64.6 5.0 %gather_fusion = f32[64,192,64]{1,2,0:T(8,128)} fusion(f32[64,192,64]{1,2,0:T(8,128)} %bitcast.57, s32[1024]{0:T(1024)S(1)} %pad_clamp_fusion.1), kind=kCustom, calls=%fused_computation | custom fusion | bytes 6291712 | tf_op jit(solution)/shard_map/gather | solution.py:40
  69.6 6.1 %copy.15 = f32[64,192,64]{2,1,0:T(8,128)} copy(f32[64,192,64]{1,2,0:T(8,128)} %gather_fusion) | data formatting | bytes 6291456 | tf_op jit(solution)/shard_map/gather | solution.py:40
  76.5 58.0 %reduce-scatter.2.cloned.1.call-done = f32[8,8,48,64]{3,2,1,0:T(8,128)} async-done(((f32[8,8,192,64]{3,2,1,0:T(8,128)}), f32[8,8,48,64]{3,2,1,0:T(8,128)}) %reduce-scatter.2.cloned.1.call-update) | async-done | bytes 786448 | tf_op jit(solution)/shard_map/reduce_scatter | solution.py:42
  134.5 2.8 %multiply_convert_fusion = bf16[8,8,48,64]{3,2,1,0:T(8,128)(2,1)} fusion(f32[48]{0:T(128)S(1)} %dynamic_slice.15, f32[8,8,48,64]{3,2,1,0:T(8,128)} %reduce-scatter.2.cloned.1.call-done), kind=kLoop, calls=%fused_computation.10 | loop fusion | flops 1572864 | bytes 1179840 | tf_op jit(solution)/shard_map/convert_element_type | solution.py:48
  137.3 29.1 %all-gather.3.cloned.1.call-done = bf16[8,8,192,64]{3,2,1,0:T(8,128)(2,1)} async-done(((bf16[8,8,48,64]{3,2,1,0:T(8,128)(2,1)}), bf16[8,8,192,64]{3,2,1,0:T(8,128)(2,1)}) %all-gather.3.cloned.1.call-update) | async-done | bytes 1572880 | tf_op jit(solution)/shard_map/all_gather | solution.py:50
  166.4 3.9 %rev.3 = bf16[8,4,2,192,64]{4,3,2,1,0:T(8,128)(2,1)} reverse(bf16[8,4,2,192,64]{4,3,2,1,0:T(8,128)(2,1)} %bitcast.59), dimensions={2} | reverse | bytes 3145728 | tf_op jit(solution)/shard_map/rev | solution.py:9
  170.3 1.8 fusion.11
  172.3 0.8 fusion.3
  173.6 1.9 scatter_custom_fusion.1
  175.5 5.2 %all-to-all-start.1 = ((bf16[8,8,3072]{2,1,0:T(8,128)(2,1)}), bf16[8,8,3072]{2,1,0:T(8,128)(2,1)S(1)}, u32[]{:S(2)}, u32[]{:S(2)}) async-start(bf16[8,8,3072]{2,1,0:T(8,128)(2,1)} %bitcast.21), calls=%async_computation.2 | async-start | bytes 786432 | tf_op jit(solution)/shard_map/all_to_all | solution.py:62
  180.7 11.2 %all-to-all-done.1 = bf16[8,8,3072]{2,1,0:T(8,128)(2,1)S(1)} async-done(((bf16[8,8,3072]{2,1,0:T(8,128)(2,1)}), bf16[8,8,3072]{2,1,0:T(8,128)(2,1)S(1)}, u32[]{:S(2)}, u32[]{:S(2)}) %all-to-all-start.1) | async-done | bytes 393248 | tf_op jit(solution)/shard_map/all_to_all | solution.py:62
  193.1 13.2 %all-gather = bf16[32,192,64]{2,1,0:T(8,128)(2,1)S(1)} all-gather(bf16[32,48,64]{2,1,0:T(8,128)(2,1)S(1)} %gather_fusion.1), channel_id=2, replica_groups=mesh['space'=8,'chan'=4] {'chan'}, dimensions={1}, use_global_device_ids=true | all-gather | bytes 983040 | tf_op jit(solution)/shard_map/all_gather | solution.py:74
  206.3 0.8 convolution_bitcast_fusion
  207.1 1.8 copy.17
  208.9 1.7 reshape.73
  210.6 2.7 %add_convert_fusion = bf16[32,24,512]{2,1,0:T(8,128)(2,1)} fusion(f32[32,24,512]{2,1,0:T(8,128)} %reshape.73, bf16[32,24,512]{2,1,0:T(8,128)(2,1)} %param.7), kind=kLoop, calls=%fused_computation.8 | loop fusion | flops 1179648 | bytes 3145728 | tf_op jit(solution)/shard_map/convert_element_type | solution.py:80
  (30 shorter events, 3.4 us)
Async XLA Ops:
  6.5 54.9 %copy-start = (bf16[8,96,192]{2,1,0:T(8,128)(2,1)S(1)}, bf16[8,96,192]{2,1,0:T(8,128)(2,1)}, u32[]{:S(2)}) copy-start(bf16[8,96,192]{2,1,0:T(8,128)(2,1)} %param.10) | copy-start | bytes 884740
  6.5 3.6 %copy-start.3 = (bf16[32,24,512]{2,1,0:T(8,128)(2,1)S(1)}, bf16[32,24,512]{2,1,0:T(8,128)(2,1)}, u32[]{:S(2)}) copy-start(bf16[32,24,512]{2,1,0:T(8,128)(2,1)} %param.7) | copy-start | bytes 2359300
  14.6 6.6 %copy-start.6 = (s32[8,8]{1,0:T(8,128)S(1)}, s32[8,8]{1,0:T(8,128)}, u32[]{:S(2)}) copy-start(s32[8,8]{1,0:T(8,128)} %param.9) | copy-start | bytes 772
  14.7 42.8 %all-to-all-start = ((bf16[8,8,24,512]{3,2,1,0:T(8,128)(2,1)}), bf16[8,8,24,512]{3,2,1,0:T(8,128)(2,1)}, u32[]{:S(2)}, u32[]{:S(2)}) async-start(bf16[8,8,24,512]{3,2,1,0:T(8,128)(2,1)} %bitcast.3), calls=%async_computation | async-start | bytes 3145728 | tf_op jit(solution)/shard_map/all_to_all | solution.py:35
  21.2 113.3 %reduce-scatter.2.cloned.1.call-start = ((), (), s32[]{:S(2)}) async-start(), calls=%async_computation.3 | async-start | bytes 7864320 | tf_op jit(solution)/shard_map/reduce_scatter | solution.py:42
  75.7 0.7 copy-start.7
  75.8 90.6 %all-gather.3.cloned.1.call-start = ((), (), s32[]{:S(2)}) async-start(), calls=%async_computation.4 | async-start | bytes 3932160 | tf_op jit(solution)/shard_map/all_gather | solution.py:50
  166.4 3.9 %copy-start.1 = (bf16[8,8,192,64]{3,2,1,0:T(8,128)(2,1)S(1)}, bf16[8,8,192,64]{3,2,1,0:T(8,128)(2,1)}, u32[]{:S(2)}) copy-start(bf16[8,8,192,64]{3,2,1,0:T(8,128)(2,1)} %all-gather.3.cloned.1.call-done) | copy-start | bytes 4718596
  170.3 1.9 copy-start.2
  170.3 1.9 copy-start.5
  175.5 16.5 %all-to-all-start.1 = ((bf16[8,8,3072]{2,1,0:T(8,128)(2,1)}), bf16[8,8,3072]{2,1,0:T(8,128)(2,1)S(1)}, u32[]{:S(2)}, u32[]{:S(2)}) async-start(bf16[8,8,3072]{2,1,0:T(8,128)(2,1)} %bitcast.21), calls=%async_computation.2 | async-start | bytes 786432 | tf_op jit(solution)/shard_map/all_to_all | solution.py:62
  192.4 13.8 %copy-start.4 = (bf16[8,192,96]{2,1,0:T(8,128)(2,1)S(1)}, bf16[8,192,96]{2,1,0:T(8,128)(2,1)}, u32[]{:S(2)}) copy-start(bf16[8,192,96]{2,1,0:T(8,128)(2,1)} %param.13) | copy-start | bytes 884740
Sparse Core Ops, SparseCore 0:
  75.9 58.5 reduce-scatter.1
  137.4 28.9 all-gather.2
where the time goes:
time: 221 us; the launch traced here: 220 us
  waiting for transfers between devices  134 us (61%)
  local copies, waits for them, and re-layouts  32.7 us (15%)
  between operations  13.5 us (6%)
  blocking collectives  13.2 us (6%)
  starting transfers between devices  11.9 us (5%)
  other arithmetic  7.91 us (4%)
  matrix products  6.57 us (3%)
    reduce_scatter x1, waiting for transfers between devices, local(): lax.psum_scatter(arranged, 'chan', scatter_dimension=2, tiled=True)  58 us
    all_to_all x1, waiting for transfers between devices, local(): lax.all_to_all(outgoing, 'space', split_axis=0, concat_axis=0, tiled=True)  36.1 us
    all_gather x1, waiting for transfers between devices, local(): incoming = lax.all_gather(coarse_act, 'chan', axis=2, tiled=True)  29.1 us
    all_gather x1, blocking collectives, local(): lax.all_gather(own_octants, 'chan', axis=1, tiled=True)  13.2 us
    all_to_all x1, waiting for transfers between devices, local(): lax.all_to_all(going_back.reshape(space_count, capacity, coarse_share * c...  11.2 us
    gather x2, local copies, waits for them, and re-layouts, local(): partial_sums.reshape(slot_count, coarse_width, cells)[parent_flat]  11.2 us
    all_to_all x1, starting transfers between devices, local(): lax.all_to_all(outgoing, 'space', split_axis=0, concat_axis=0, tiled=True)  6.55 us
    all_to_all x1, starting transfers between devices, local(): lax.all_to_all(going_back.reshape(space_count, capacity, coarse_share * c...  5.24 us
  transfers between devices with their start and end apart: 4, of which 4 were waited for; matrix products, arithmetic and copies ran while one was open for 0% of the time, Pallas kernels for 0%

commit v1 on v0

v1 whole, which is shorter than its diff:
```python
import functools

import jax
import jax.numpy as jnp
from jax import lax
from jax.experimental import pallas as pl
from jax.experimental.pallas import tpu as pltpu
from jax.sharding import PartitionSpec as P

MESH = pl.DeviceIdType.MESH
LANES = 128
ROWS = 16
BF16 = jnp.bfloat16
F32 = jnp.float32


def route_kernel(capacity, route_ref, slots_ref, block_of, partner_of, slot_of, count):
    blocks = route_ref.shape[0]
    pairs = blocks // 2
    slot_count = block_of.shape[0]
    half = slot_count // 2

    def clear(t, carry):
        block_of[t] = 2 * pairs
        return carry

    lax.fori_loop(0, slot_count, clear, 0, unroll=8)

    def clear_count(d, carry):
        count[d] = 0
        return carry

    lax.fori_loop(0, count.shape[0], clear_count, 0, unroll=8)

    def place(j, carry):
        d = route_ref[j, 0]
        r = count[d]
        count[d] = r + 1
        slot = d * capacity + r
        block_of[slot] = (j % 2) * pairs + j // 2
        slot_of[j] = (slot % 2) * half + slot // 2
        return carry

    lax.fori_loop(0, blocks, place, 0, unroll=4)

    def pair(g, carry):
        for q in range(0, 8, 2):
            a = slots_ref[g, q]
            b = slots_ref[g, q + 1]
            partner_of[a] = (b % 2) * half + b // 2
            partner_of[b] = (a % 2) * half + a // 2
        return carry

    lax.fori_loop(0, slots_ref.shape[0], pair, 0, unroll=2)


def main_kernel(
    n, capacity, block_of, partner_of, slot_of, tiles, w_down, bias, w_mid, w_up, out,
    down_t, mid_t, up_t, bias_t, part, core_in, x_out, x_in, acts, going, arrived, twice,
    back, returned, again, full, core_s, core_r, x_s, x_r, go_s, go_r, back_s, back_r,
    share_s, share_r, all_s, all_r,
):
    blocks, fine_share, voxels = tiles.shape
    pairs = blocks // 2
    width = w_down.shape[2]
    chunks = part.shape[1]
    per_dest = capacity // 2
    half = n * per_dest
    me = lax.axis_index("space")
    rank = lax.axis_index("chan")
    hi, lo = rank // 2, rank % 2
    core_peer = 2 * hi + 1 - lo
    x_peer = 2 * (1 - hi) + lo

    barrier = pltpu.get_barrier_semaphore()

    def greet(off, carry):
        pl.semaphore_signal(
            barrier, inc=1, device_id=(lax.rem(me + off, n), rank), device_id_type=MESH
        )
        return carry

    lax.fori_loop(1, n, greet, 0)
    for peer in (core_peer, x_peer):
        pl.semaphore_signal(barrier, inc=1, device_id=(me, peer), device_id_type=MESH)

    left = lax.broadcasted_iota(jnp.int32, (1, LANES), 1) < LANES // 2

    def swap(v):
        return pltpu.roll(v, LANES // 2, 1)

    pad = 32
    row = lax.broadcasted_iota(jnp.int32, (pad, w_down.shape[1]), 0)
    col = lax.broadcasted_iota(jnp.int32, (pad, w_down.shape[1]), 1)
    pick = jnp.where((row < fine_share) & (col == rank * fine_share + row), 1.0, 0.0).astype(BF16)
    for parity in range(2):
        stacked = jnp.concatenate(
            [
                jnp.dot(pick, w_down[2 * a + parity], preferred_element_type=F32)
                for a in range(4)
            ],
            axis=0,
        )
        down_t[parity] = stacked.T.astype(BF16)

    zeros = jnp.zeros((pad - fine_share, LANES), F32)

    def down(step, carry):
        columns = []
        for b in range(4):
            tile = tiles[step * 4 + b].astype(F32)
            pieces = []
            for a in range(4):
                pieces += [tile[:, a * LANES : (a + 1) * LANES], zeros]
            columns.append(jnp.concatenate(pieces, axis=0).astype(BF16))
        x = jnp.concatenate(columns, axis=1)
        even = jnp.dot(down_t[0], x, preferred_element_type=F32)
        odd = jnp.dot(down_t[1], x, preferred_element_type=F32)
        for u in range(2):
            e0, e1 = even[:, 2 * u * LANES :][:, :LANES], even[:, (2 * u + 1) * LANES :][:, :LANES]
            o0, o1 = odd[:, 2 * u * LANES :][:, :LANES], odd[:, (2 * u + 1) * LANES :][:, :LANES]
            both = (jnp.where(left, e0, o1) + swap(jnp.where(left, e1, o0))).astype(BF16)
            for h in range(2):
                for l in range(2):
                    for ch in range(chunks):
                        at = (2 * h + l) * chunks * ROWS + ch * ROWS
                        part[l, ch, h, step * 2 + u] = both[at : at + ROWS]
        return carry

    lax.fori_loop(0, blocks // 4, down, 0)

    pl.semaphore_wait(barrier, n + 1)

    def to(src, dst, send, recv, space, chan):
        return pltpu.make_async_remote_copy(
            src_ref=src, dst_ref=dst, send_sem=send, recv_sem=recv,
            device_id=(space, chan), device_id_type=MESH,
        )

    cores = [
        to(part.at[1 - lo, ch], core_in.at[ch], core_s.at[ch], core_r.at[ch], me, core_peer)
        for ch in range(chunks)
    ]
    for copy in cores:
        copy.start()

    bias_t[...] = jnp.broadcast_to(bias[...], (LANES, width)).T.reshape(
        4 * chunks, ROWS, LANES
    )

    xs = [to(x_out.at[ch], x_in.at[ch], x_s.at[ch], x_r.at[ch], me, x_peer) for ch in range(chunks)]
    for ch in range(chunks):
        cores[ch].wait_recv()
        x_out[ch] = (
            part[lo, ch, 1 - hi].astype(F32) + core_in[ch, 1 - hi].astype(F32)
        ).astype(BF16)
        xs[ch].start()

    def silu(v):
        return v / (1.0 + jnp.exp(-v))

    def spread(ref, ch, flat, count):
        swapped = swap(flat)
        ref[ch, 0:count] = jnp.where(left, flat, swapped).astype(BF16).reshape(count, ROWS, LANES)
        ref[ch, count : 2 * count] = (
            jnp.where(left, swapped, flat).astype(BF16).reshape(count, ROWS, LANES)
        )

    def joined(ref, ch, first, second):
        return jnp.where(left, ref[ch, first].astype(F32), ref[ch, second].astype(F32))

    def exchange(src, dst, send, recv, ch, d):
        return to(src.at[ch, d], dst.at[ch, me], send.at[ch], recv.at[ch], d, rank)

    other = lax.rem(me + 1, n)

    def whole(src, dst, send, recv, ch):
        return to(
            src.at[ch, pl.ds(0, n - 1)], dst.at[ch, pl.ds(0, n - 1)], send.at[ch], recv.at[ch],
            other, rank,
        )

    for ch in range(chunks):
        xs[ch].wait_recv()
        b = bias_t[rank * chunks + ch]
        total = (
            part[lo, ch, hi].astype(F32)
            + core_in[ch, hi].astype(F32)
            + x_in[ch].astype(F32)
            + b[None]
        )
        spread(acts, ch, silu(total).reshape(pairs * ROWS, LANES), pairs)
        acts[ch, 2 * pairs] = silu(b).astype(BF16)

        def send(off, carry, ch=ch):
            d = lax.rem(me + off, n)
            for m in range(per_dest):
                t = d * capacity + 2 * m
                going[ch, d, m] = joined(acts, ch, block_of[t], block_of[t + 1]).astype(BF16)
            exchange(going, arrived, go_s, go_r, ch, d).start()
            return carry

        lax.fori_loop(1, n, send, 0)
        for m in range(per_dest):
            t = me * capacity + 2 * m
            arrived[ch, me, m] = joined(acts, ch, block_of[t], block_of[t + 1]).astype(BF16)

    row = lax.broadcasted_iota(jnp.int32, (fine_share, w_up.shape[2]), 0)
    col = lax.broadcasted_iota(jnp.int32, (fine_share, w_up.shape[2]), 1)
    pick_up = jnp.where(col == rank * fine_share + row, 1.0, 0.0).astype(BF16)
    up_t[...] = jnp.concatenate(
        [
            lax.dot_general(
                pick_up, w_up[o], (((1,), (1,)), ((), ())), preferred_element_type=F32
            )
            for o in range(8)
        ],
        axis=0,
    ).astype(BF16)
    mid = w_mid[...].astype(F32)
    ordered = []
    for l in range(2):
        for ch in range(chunks):
            for h in range(2):
                at = (2 * h + l) * chunks * ROWS + ch * ROWS
                ordered.append(mid[at : at + ROWS])
    mid_t[...] = jnp.concatenate(ordered, axis=0).T.astype(BF16)

    for ch in range(chunks):
        whole(going, arrived, go_s, go_r, ch).wait_recv()
        spread(
            twice, ch, arrived[ch].astype(F32).reshape(half * ROWS, LANES), half
        )

        def paired(d, ch=ch):
            sums = []
            for m in range(per_dest):
                t = d * capacity + 2 * m
                own = arrived[ch, d, m].astype(F32)
                sums.append(
                    (own + joined(twice, ch, partner_of[t], partner_of[t + 1])).astype(BF16)
                )
            return sums

        def send_back(off, carry, ch=ch, paired=paired):
            d = lax.rem(me + off, n)
            for m, value in enumerate(paired(d)):
                back[ch, d, m] = value
            exchange(back, returned, back_s, back_r, ch, d).start()
            return carry

        lax.fori_loop(1, n, send_back, 0)
        for m, value in enumerate(paired(me)):
            returned[ch, me, m] = value

    shares = [
        to(full.at[lo, ch, hi], full.at[lo, ch, hi], share_s.at[ch], share_r.at[ch], me, x_peer)
        for ch in range(chunks)
    ]
    alls = [
        to(full.at[lo, ch], full.at[lo, ch], all_s.at[ch], all_r.at[ch], me, core_peer)
        for ch in range(chunks)
    ]
    for ch in range(chunks):
        whole(back, returned, back_s, back_r, ch).wait_recv()
        spread(
            again, ch, returned[ch].astype(F32).reshape(half * ROWS, LANES), half
        )

        def collect(m, carry, ch=ch):
            full[lo, ch, hi, m] = joined(again, ch, slot_of[2 * m], slot_of[2 * m + 1]).astype(BF16)
            return carry

        lax.fori_loop(0, pairs, collect, 0, unroll=4)
        shares[ch].start()
    for ch in range(chunks):
        shares[ch].wait_recv()
        alls[ch].start()
    for ch in range(chunks):
        alls[ch].wait_recv()

    def up(step, carry):
        x = jnp.concatenate(
            [full[:, :, :, step * 2 + u].reshape(width, LANES) for u in range(2)], axis=1
        )
        coarse = jnp.dot(mid_t[...], x, preferred_element_type=F32).astype(BF16)
        lifted = jnp.dot(up_t[...], coarse, preferred_element_type=F32)
        for u in range(2):
            mine = lifted[:, u * LANES : (u + 1) * LANES]
            swapped = swap(mine)
            for b in range(2):
                j = step * 4 + 2 * u + b
                first, second = (mine, swapped) if b == 0 else (swapped, mine)
                for a in range(4):
                    r0, r1 = 2 * a * fine_share, (2 * a + 1) * fine_share
                    value = jnp.where(
                        left, first[r0 : r0 + fine_share], second[r1 : r1 + fine_share]
                    )
                    at = pl.ds(a * LANES, LANES)
                    out[j, :, at] = (tiles[j, :, at].astype(F32) + value).astype(BF16)
        return carry

    lax.fori_loop(0, pairs // 2, up, 0)

    for ch in range(chunks):
        cores[ch].wait_send()
        xs[ch].wait_send()
        whole(going, arrived, go_s, go_r, ch).wait_send()
        whole(back, returned, back_s, back_r, ch).wait_send()
        shares[ch].wait_send()
        alls[ch].wait_send()


def local(fine_tiles, parent_route, parent_slots, w_down, coarse_bias, w_mid, w_up):
    n = lax.axis_size("space")
    blocks = fine_tiles.shape[0]
    pairs = blocks // 2
    width = w_down.shape[2]
    slot_count = parent_slots.shape[0] * 8
    capacity = slot_count // n
    per_dest = capacity // 2
    half = slot_count // 2
    chunks = width // (4 * ROWS)
    smem = pl.BlockSpec(memory_space=pltpu.SMEM)
    vmem = pl.BlockSpec(memory_space=pltpu.VMEM)
    ints = jax.ShapeDtypeStruct((slot_count,), jnp.int32)
    tables = pl.pallas_call(
        functools.partial(route_kernel, capacity),
        out_shape=(ints, ints, jax.ShapeDtypeStruct((blocks,), jnp.int32)),
        in_specs=[smem, smem],
        out_specs=(smem, smem, smem),
        scratch_shapes=[pltpu.SMEM((n,), jnp.int32)],
    )(parent_route, parent_slots)

    def buffer(*shape):
        return pltpu.VMEM(shape + (ROWS, LANES), BF16)

    return pl.pallas_call(
        functools.partial(main_kernel, n, capacity),
        out_shape=jax.ShapeDtypeStruct(fine_tiles.shape, fine_tiles.dtype),
        in_specs=[smem] * 3 + [vmem] * 5,
        out_specs=vmem,
        scratch_shapes=[
            pltpu.VMEM((2, width, LANES), BF16),
            pltpu.VMEM((width, width), BF16),
            pltpu.VMEM((8 * fine_tiles.shape[1], width), BF16),
            pltpu.VMEM((4 * chunks, ROWS, LANES), F32),
            buffer(2, chunks, 2, pairs),
            buffer(chunks, 2, pairs),
            buffer(chunks, pairs),
            buffer(chunks, pairs),
            buffer(chunks, 2 * pairs + 1),
            buffer(chunks, n, per_dest),
            buffer(chunks, n, per_dest),
            buffer(chunks, 2 * half),
            buffer(chunks, n, per_dest),
            buffer(chunks, n, per_dest),
            buffer(chunks, 2 * half),
            buffer(2, chunks, 2, pairs),
        ]
        + [pltpu.SemaphoreType.DMA((chunks,))] * 12,
        compiler_params=pltpu.CompilerParams(
            collective_id=0, has_side_effects=True, vmem_limit_bytes=32 * 1024 * 1024
        ),
    )(*tables, fine_tiles, w_down, coarse_bias.reshape(1, width), w_mid, w_up)


def solution(mesh):
    in_specs = (P("space", "chan", None), P("space", None), P("space", None), P(), P(), P(), P())
    out_specs = P("space", "chan", None)
    return jax.shard_map(local, mesh=mesh, in_specs=in_specs, out_specs=out_specs, check_vma=False)
```

time: 221 us -> 48.5 us (0.22)
  waiting for transfers between devices: 134 us -> 0 us
  Pallas kernels: 0 us -> 41.2 us
  local copies, waits for them, and re-layouts: 32.7 us -> 6.91 us
  between operations: 13.5 us -> 0.06 us
  blocking collectives: 13.2 us -> 0 us
  starting transfers between devices: 11.9 us -> 0 us
  other arithmetic: 7.91 us -> 0 us
  matrix products: 6.57 us -> 0 us
    reduce_scatter x1 -> x0, waiting for transfers between devices: 58 us -> none  [local(): lax.psum_scatter(arranged, 'chan', scatter_dimension=2, tiled=True)]
    all_to_all x2 -> x0, waiting for transfers between devices: 47.3 us -> none  [the longest x1 36.1 us: local(): lax.all_to_all(outgoing, 'space', split_axis=0, concat_axis=0, tiled=True)]
    pallas_call x0 -> x2, Pallas kernels: none -> 41.2 us  [the longest x1 38.6 us: local(): pl.pallas_call(functools.partial(main_kernel, n, capacity), out_shape=jax...]
    all_gather x1 -> x0, waiting for transfers between devices: 29.1 us -> none  [local(): incoming = lax.all_gather(coarse_act, 'chan', axis=2, tiled=True)]
    all_gather x1 -> x0, blocking collectives: 13.2 us -> none  [local(): lax.all_gather(own_octants, 'chan', axis=1, tiled=True)]
    all_to_all x2 -> x0, starting transfers between devices: 11.8 us -> none  [the longest x1 6.55 us: local(): lax.all_to_all(outgoing, 'space', split_axis=0, concat_axis=0, tiled=True)]
    gather x3 -> x0, local copies, waits for them, and re-layouts: 11.8 us -> none  [the longest x2 11.2 us: local(): partial_sums.reshape(slot_count, coarse_width, cells)[parent_flat]]
    reshape x5 -> x0, local copies, waits for them, and re-layouts: 6.74 us -> none  [the longest x1 3.94 us: local(): arrived.reshape(arrived.shape[0], arrived.shape[1], fine_share, 8, cells)]
  transfers between devices with their start and end apart: 4 -> 0, of which waited for: 4 -> 0; matrix products, arithmetic and copies ran while one was open for 0% -> 0% of each run, Pallas kernels for 0% -> 0%
where the time goes in v1:
time: 48.5 us; the launch traced here: 48.1 us
  Pallas kernels  41.2 us (85%)
  local copies, waits for them, and re-layouts  6.91 us (14%)
    pallas_call x1, Pallas kernels, local(): pl.pallas_call(functools.partial(main_kernel, n, capacity), out_shape=jax...  38.6 us
    unnamed x20, local copies, waits for them, and re-layouts  6.91 us
    pallas_call x1, Pallas kernels, local(): pl.pallas_call(functools.partial(route_kernel, capacity), out_shape=(ints...  2.54 us

profile of v1, /device:TPU:1, one launch (start us, length us, event | category | flops | bytes accessed | tf_op | source)
XLA Modules:
  0.0 48.1 jit_solution(12521209522210201422)
XLA Ops:
  0.0 0.0 copy-start.8
  0.0 0.7 %copy-done.8 = s32[32,1]{0,1:T(1,128)S(1)} copy-done((s32[32,1]{0,1:T(1,128)S(1)}, s32[32,1]{0,1:T(1,128)}, u32[]{:S(2)}) %copy-start.8) | copy-done | bytes 152
  0.7 0.7 %copy.8.route_ref = s32[32,1]{1,0:T(8,128)} copy(s32[32,1]{0,1:T(1,128)S(1)} %copy-done.8) | data formatting | bytes 256 | tf_op args[1]
  1.3 2.5 %shard_map.73 = (s32[64]{0:T(128)}, s32[64]{0:T(128)}, s32[32]{0:T(128)}) custom-call(s32[32,1]{1,0:T(8,128)} %copy.8.route_ref, s32[8,8]{1,0:T(8,128)} %slots_ref.1), custom_call_target="tpu_custom_call" | custom-call | tf_op jit(solution)/shard_map/pallas_call | solution.py:327
  3.9 0.0 copy-start.6
  3.9 0.0 copy-start.7
  3.9 0.0 copy-start.4
  3.9 0.0 copy-start.5
  3.9 0.6 %copy-done.6 = s32[64]{0:T(128)S(1)} copy-done((s32[64]{0:T(128)S(1)}, s32[64]{0:T(128)}, u32[]{:S(2)}) %copy-start.6) | copy-done | bytes 280
  4.5 0.1 copy-done.7
  4.6 0.0 copy-done.4
  4.6 0.0 copy-done.5
  4.6 0.0 copy-start
  4.6 1.1 %copy-done = bf16[32,24,512]{2,1,0:T(8,128)(2,1)S(1)} copy-done((bf16[32,24,512]{2,1,0:T(8,128)(2,1)S(1)}, bf16[32,24,512]{2,1,0:T(8,128)(2,1)}, u32[]{:S(2)}) %copy-start) | copy-done | bytes 786456
  5.7 0.0 copy-start.1
  5.7 1.0 %copy-done.1 = bf16[8,96,192]{2,1,0:T(8,128)(2,1)S(1)} copy-done((bf16[8,96,192]{2,1,0:T(8,128)(2,1)S(1)}, bf16[8,96,192]{2,1,0:T(8,128)(2,1)}, u32[]{:S(2)}) %copy-start.1) | copy-done | bytes 294936
  6.7 0.0 copy-start.2
  6.7 1.0 %copy-done.2 = bf16[8,192,96]{2,1,0:T(8,128)(2,1)S(1)} copy-done((bf16[8,192,96]{2,1,0:T(8,128)(2,1)S(1)}, bf16[8,192,96]{2,1,0:T(8,128)(2,1)}, u32[]{:S(2)}) %copy-start.2) | copy-done | bytes 294936
  7.7 0.0 copy-start.3
  7.7 0.9 %copy-done.3 = bf16[192,192]{1,0:T(8,128)(2,1)S(1)} copy-done((bf16[192,192]{1,0:T(8,128)(2,1)S(1)}, bf16[192,192]{1,0:T(8,128)(2,1)}, u32[]{:S(2)}) %copy-start.3) | copy-done | bytes 73752
  8.6 38.6 %shard_map.74 = bf16[32,24,512]{2,1,0:T(8,128)(2,1)S(1)} custom-call(s32[64]{0:T(128)S(1)} %copy-done.5, s32[64]{0:T(128)S(1)} %copy-done.6, s32[32]{0:T(128)S(1)} %copy-done.7, bf16[32,24,512]{2,1,0:T(8,128)(2,1)S(1)} %copy-done, bf16[8,96,192]{2,1,0:T(8,128)(2,1)S(1)} %copy-done.1, f32[1,192]{1,0:T(1,128)S(1)} %bitcast.1, bf16[192,192]{1,0:T(8,128)(2,1)S(1)} %copy-done.3, ...), custom_call_target="tpu_custom_call" | custom-call | tf_op jit(solution)/shard_map/pallas_call | solution.py:338
  47.2 0.9 %copy.10 = bf16[32,24,512]{2,1,0:T(8,128)(2,1)} copy(bf16[32,24,512]{2,1,0:T(8,128)(2,1)S(1)} %shard_map.74) | data formatting | bytes 1572864
Async XLA Ops:
  0.0 0.7 %copy-start.8 = (s32[32,1]{0,1:T(1,128)S(1)}, s32[32,1]{0,1:T(1,128)}, u32[]{:S(2)}) copy-start(s32[32,1]{0,1:T(1,128)} %param.8) | copy-start | bytes 388
  3.9 0.6 %copy-start.6 = (s32[64]{0:T(128)S(1)}, s32[64]{0:T(128)}, u32[]{:S(2)}) copy-start(s32[64]{0:T(128)} %get-tuple-element.9.partner_of) | copy-start | bytes 772
  3.9 0.7 %copy-start.7 = (s32[32]{0:T(128)S(1)}, s32[32]{0:T(128)}, u32[]{:S(2)}) copy-start(s32[32]{0:T(128)} %get-tuple-element.10.slot_of) | copy-start | bytes 388
  3.9 0.7 %copy-start.4 = (f32[192]{0:T(256)S(1)}, f32[192]{0:T(256)}, u32[]{:S(2)}) copy-start(f32[192]{0:T(256)} %param.11) | copy-start | bytes 2308
  3.9 0.7 %copy-start.5 = (s32[64]{0:T(128)S(1)}, s32[64]{0:T(128)}, u32[]{:S(2)}) copy-start(s32[64]{0:T(128)} %get-tuple-element.8.block_of) | copy-start | bytes 772
  4.6 1.1 %copy-start = (bf16[32,24,512]{2,1,0:T(8,128)(2,1)S(1)}, bf16[32,24,512]{2,1,0:T(8,128)(2,1)}, u32[]{:S(2)}) copy-start(bf16[32,24,512]{2,1,0:T(8,128)(2,1)} %tiles.1) | copy-start | bytes 2359300
  5.7 1.0 %copy-start.1 = (bf16[8,96,192]{2,1,0:T(8,128)(2,1)S(1)}, bf16[8,96,192]{2,1,0:T(8,128)(2,1)}, u32[]{:S(2)}) copy-start(bf16[8,96,192]{2,1,0:T(8,128)(2,1)} %w_down.1) | copy-start | bytes 884740
  6.7 1.0 %copy-start.2 = (bf16[8,192,96]{2,1,0:T(8,128)(2,1)S(1)}, bf16[8,192,96]{2,1,0:T(8,128)(2,1)}, u32[]{:S(2)}) copy-start(bf16[8,192,96]{2,1,0:T(8,128)(2,1)} %w_up.1) | copy-start | bytes 884740
  7.7 0.9 %copy-start.3 = (bf16[192,192]{1,0:T(8,128)(2,1)S(1)}, bf16[192,192]{1,0:T(8,128)(2,1)}, u32[]{:S(2)}) copy-start(bf16[192,192]{1,0:T(8,128)(2,1)} %w_mid.1) | copy-start | bytes 221188

commit v2 on v1

--- a/solution.py
+++ b/solution.py
@@ -14,53 +14,55 @@
 F32 = jnp.float32
 
 
-def route_kernel(capacity, route_ref, slots_ref, block_of, partner_of, slot_of, count):
-    blocks = route_ref.shape[0]
+def build_tables(n, capacity, route, slots, tables):
+    blocks = route.shape[1]
     pairs = blocks // 2
-    slot_count = block_of.shape[0]
-    half = slot_count // 2
-
-    def clear(t, carry):
-        block_of[t] = 2 * pairs
-        return carry
-
-    lax.fori_loop(0, slot_count, clear, 0, unroll=8)
-
-    def clear_count(d, carry):
-        count[d] = 0
-        return carry
-
-    lax.fori_loop(0, count.shape[0], clear_count, 0, unroll=8)
-
-    def place(j, carry):
-        d = route_ref[j, 0]
-        r = count[d]
-        count[d] = r + 1
-        slot = d * capacity + r
-        block_of[slot] = (j % 2) * pairs + j // 2
-        slot_of[j] = (slot % 2) * half + slot // 2
-        return carry
-
-    lax.fori_loop(0, blocks, place, 0, unroll=4)
-
-    def pair(g, carry):
-        for q in range(0, 8, 2):
-            a = slots_ref[g, q]
-            b = slots_ref[g, q + 1]
-            partner_of[a] = (b % 2) * half + b // 2
-            partner_of[b] = (a % 2) * half + a // 2
-        return carry
-
-    lax.fori_loop(0, slots_ref.shape[0], pair, 0, unroll=2)
+    half = n * capacity // 2
+    lanes = tables.shape[1]
+
+    def place(slot):
+        return (slot % 2) * half + slot // 2
+
+    j_row = lax.broadcasted_iota(jnp.int32, (blocks, blocks), 0)
+    j_col = lax.broadcasted_iota(jnp.int32, (blocks, blocks), 1)
+    row = jnp.broadcast_to(route[...], (blocks, blocks))
+    own = jnp.sum(jnp.where(j_row == j_col, row, 0), axis=1, keepdims=True)
+    earlier = jnp.where((row == own) & (j_col < j_row), 1, 0)
+    slot = own * capacity + jnp.sum(earlier, axis=1, keepdims=True)
+    j = lax.broadcasted_iota(jnp.int32, (blocks, lanes), 0)
+    t = lax.broadcasted_iota(jnp.int32, (blocks, lanes), 1)
+    named = jnp.where(slot == t, (j % 2) * pairs + j // 2 - 2 * pairs, 0)
+    tables[...] = jnp.zeros_like(tables)
+    tables[0:1] = jnp.sum(named, axis=0, keepdims=True) + 2 * pairs
+    tables[2:3] = jnp.sum(jnp.where(j == t, place(slot), 0), axis=0, keepdims=True)
+    t = lax.broadcasted_iota(jnp.int32, (slots.shape[0], lanes), 1)
+    partner = jnp.zeros((slots.shape[0], lanes), jnp.int32)
+    for q in range(8):
+        mate = q + 1 - 2 * (q % 2)
+        partner += jnp.where(slots[:, q : q + 1] == t, place(slots[:, mate : mate + 1]), 0)
+    tables[1:2] = jnp.sum(partner, axis=0, keepdims=True)
 
 
 def main_kernel(
-    n, capacity, block_of, partner_of, slot_of, tiles, w_down, bias, w_mid, w_up, out,
+    n, capacity, route_in, slots_in, tiles_in, down_in, bias_in, mid_in, up_in, out,
+    tiles, w_down, bias, w_mid, w_up, route, slots, tables, index, load_s, store_s, table_s,
     down_t, mid_t, up_t, bias_t, part, core_in, x_out, x_in, acts, going, arrived, twice,
     back, returned, again, full, core_s, core_r, x_s, x_r, go_s, go_r, back_s, back_r,
     share_s, share_r, all_s, all_r,
 ):
     blocks, fine_share, voxels = tiles.shape
+    pieces_in = 4
+    piece = blocks // pieces_in
+    sources = [(down_in, w_down), (route_in, route), (slots_in, slots)]
+    for p in range(pieces_in):
+        at = pl.ds(p * piece, piece)
+        sources.append((tiles_in.at[at], tiles.at[at]))
+    sources += [(bias_in, bias), (mid_in, w_mid), (up_in, w_up)]
+    loads = [
+        pltpu.make_async_copy(src, dst, load_s.at[i]) for i, (src, dst) in enumerate(sources)
+    ]
+    for load in loads:
+        load.start()
     pairs = blocks // 2
     width = w_down.shape[2]
     chunks = part.shape[1]
@@ -92,6 +94,12 @@
     pad = 32
     row = lax.broadcasted_iota(jnp.int32, (pad, w_down.shape[1]), 0)
     col = lax.broadcasted_iota(jnp.int32, (pad, w_down.shape[1]), 1)
+    loads[1].wait()
+    loads[2].wait()
+    build_tables(n, capacity, route, slots, tables)
+    table_copy = pltpu.make_async_copy(tables, index, table_s)
+    table_copy.start()
+    loads[0].wait()
     pick = jnp.where((row < fine_share) & (col == rank * fine_share + row), 1.0, 0.0).astype(BF16)
     for parity in range(2):
         stacked = jnp.concatenate(
@@ -127,7 +135,9 @@
                         part[l, ch, h, step * 2 + u] = both[at : at + ROWS]
         return carry
 
-    lax.fori_loop(0, blocks // 4, down, 0)
+    for p in range(pieces_in):
+        loads[3 + p].wait()
+        lax.fori_loop(p * piece // 4, (p + 1) * piece // 4, down, 0)
 
     pl.semaphore_wait(barrier, n + 1)
 
@@ -144,6 +154,7 @@
     for copy in cores:
         copy.start()
 
+    loads[3 + pieces_in].wait()
     bias_t[...] = jnp.broadcast_to(bias[...], (LANES, width)).T.reshape(
         4 * chunks, ROWS, LANES
     )
@@ -180,6 +191,7 @@
             other, rank,
         )
 
+    table_copy.wait()
     for ch in range(chunks):
         xs[ch].wait_recv()
         b = bias_t[rank * chunks + ch]
@@ -196,15 +208,17 @@
             d = lax.rem(me + off, n)
             for m in range(per_dest):
                 t = d * capacity + 2 * m
-                going[ch, d, m] = joined(acts, ch, block_of[t], block_of[t + 1]).astype(BF16)
+                going[ch, d, m] = joined(acts, ch, index[0, t], index[0, t + 1]).astype(BF16)
             exchange(going, arrived, go_s, go_r, ch, d).start()
             return carry
 
         lax.fori_loop(1, n, send, 0)
         for m in range(per_dest):
             t = me * capacity + 2 * m
-            arrived[ch, me, m] = joined(acts, ch, block_of[t], block_of[t + 1]).astype(BF16)
-
+            arrived[ch, me, m] = joined(acts, ch, index[0, t], index[0, t + 1]).astype(BF16)
+
+    loads[4 + pieces_in].wait()
+    loads[5 + pieces_in].wait()
     row = lax.broadcasted_iota(jnp.int32, (fine_share, w_up.shape[2]), 0)
     col = lax.broadcasted_iota(jnp.int32, (fine_share, w_up.shape[2]), 1)
     pick_up = jnp.where(col == rank * fine_share + row, 1.0, 0.0).astype(BF16)
@@ -238,7 +252,7 @@
                 t = d * capacity + 2 * m
                 own = arrived[ch, d, m].astype(F32)
                 sums.append(
-                    (own + joined(twice, ch, partner_of[t], partner_of[t + 1])).astype(BF16)
+                    (own + joined(twice, ch, index[1, t], index[1, t + 1])).astype(BF16)
                 )
             return sums
 
@@ -268,7 +282,7 @@
         )
 
         def collect(m, carry, ch=ch):
-            full[lo, ch, hi, m] = joined(again, ch, slot_of[2 * m], slot_of[2 * m + 1]).astype(BF16)
+            full[lo, ch, hi, m] = joined(again, ch, index[2, 2 * m], index[2, 2 * m + 1]).astype(BF16)
             return carry
 
         lax.fori_loop(0, pairs, collect, 0, unroll=4)
@@ -297,10 +311,15 @@
                         left, first[r0 : r0 + fine_share], second[r1 : r1 + fine_share]
                     )
                     at = pl.ds(a * LANES, LANES)
-                    out[j, :, at] = (tiles[j, :, at].astype(F32) + value).astype(BF16)
+                    tiles[j, :, at] = (tiles[j, :, at].astype(F32) + value).astype(BF16)
         return carry
 
-    lax.fori_loop(0, pairs // 2, up, 0)
+    stores = []
+    for p in range(pieces_in):
+        lax.fori_loop(p * piece // 4, (p + 1) * piece // 4, up, 0)
+        at = pl.ds(p * piece, piece)
+        stores.append(pltpu.make_async_copy(tiles.at[at], out.at[at], store_s.at[p]))
+        stores[p].start()
 
     for ch in range(chunks):
         cores[ch].wait_send()
@@ -309,6 +328,8 @@
         whole(back, returned, back_s, back_r, ch).wait_send()
         shares[ch].wait_send()
         alls[ch].wait_send()
+    for store in stores:
+        store.wait()
 
 
 def local(fine_tiles, parent_route, parent_slots, w_down, coarse_bias, w_mid, w_up):
@@ -321,16 +342,8 @@
     per_dest = capacity // 2
     half = slot_count // 2
     chunks = width // (4 * ROWS)
-    smem = pl.BlockSpec(memory_space=pltpu.SMEM)
-    vmem = pl.BlockSpec(memory_space=pltpu.VMEM)
-    ints = jax.ShapeDtypeStruct((slot_count,), jnp.int32)
-    tables = pl.pallas_call(
-        functools.partial(route_kernel, capacity),
-        out_shape=(ints, ints, jax.ShapeDtypeStruct((blocks,), jnp.int32)),
-        in_specs=[smem, smem],
-        out_specs=(smem, smem, smem),
-        scratch_shapes=[pltpu.SMEM((n,), jnp.int32)],
-    )(parent_route, parent_slots)
+    hbm = pl.BlockSpec(memory_space=pltpu.HBM)
+    lanes = -(-max(slot_count, blocks) // LANES) * LANES
 
     def buffer(*shape):
         return pltpu.VMEM(shape + (ROWS, LANES), BF16)
@@ -338,9 +351,21 @@
     return pl.pallas_call(
         functools.partial(main_kernel, n, capacity),
         out_shape=jax.ShapeDtypeStruct(fine_tiles.shape, fine_tiles.dtype),
-        in_specs=[smem] * 3 + [vmem] * 5,
-        out_specs=vmem,
+        in_specs=[hbm] * 7,
+        out_specs=hbm,
         scratch_shapes=[
+            pltpu.VMEM(fine_tiles.shape, BF16),
+            pltpu.VMEM(w_down.shape, BF16),
+            pltpu.VMEM((1, width), F32),
+            pltpu.VMEM(w_mid.shape, BF16),
+            pltpu.VMEM(w_up.shape, BF16),
+            pltpu.VMEM((1, blocks), jnp.int32),
+            pltpu.VMEM(parent_slots.shape, jnp.int32),
+            pltpu.VMEM((8, lanes), jnp.int32),
+            pltpu.SMEM((8, lanes), jnp.int32),
+            pltpu.SemaphoreType.DMA((10,)),
+            pltpu.SemaphoreType.DMA((4,)),
+            pltpu.SemaphoreType.DMA,
             pltpu.VMEM((2, width, LANES), BF16),
             pltpu.VMEM((width, width), BF16),
             pltpu.VMEM((8 * fine_tiles.shape[1], width), BF16),
@@ -360,9 +385,17 @@
         ]
         + [pltpu.SemaphoreType.DMA((chunks,))] * 12,
         compiler_params=pltpu.CompilerParams(
-            collective_id=0, has_side_effects=True, vmem_limit_bytes=32 * 1024 * 1024
+            collective_id=0, has_side_effects=True, vmem_limit_bytes=62 * 1024 * 1024
         ),
-    )(*tables, fine_tiles, w_down, coarse_bias.reshape(1, width), w_mid, w_up)
+    )(
+        parent_route.reshape(1, blocks),
+        parent_slots,
+        fine_tiles,
+        w_down,
+        coarse_bias.reshape(1, width),
+        w_mid,
+        w_up,
+    )
 
 
 def solution(mesh):

time: 48.5 us -> 42 us (0.87)
  local copies, waits for them, and re-layouts: 6.91 us -> 2.06 us
  Pallas kernels: 41.2 us -> 39.8 us
    unnamed x20 -> x1, local copies, waits for them, and re-layouts: 6.91 us -> 2.06 us
    pallas_call x1 -> x0, Pallas kernels: 2.54 us -> none  [local(): pl.pallas_call(functools.partial(route_kernel, capacity), out_shape=(ints...]
    pallas_call x1, Pallas kernels: 38.6 us -> 39.8 us  [local(): pl.pallas_call(functools.partial(main_kernel, n, capacity), out_shape=jax...]
where the time goes in v2:
time: 42 us; the launch traced here: 41.9 us
  Pallas kernels  39.8 us (95%)
  local copies, waits for them, and re-layouts  2.06 us (5%)
    pallas_call x1, Pallas kernels, local(): pl.pallas_call(functools.partial(main_kernel, n, capacity), out_shape=jax...  39.8 us
    unnamed x1, local copies, waits for them, and re-layouts  2.06 us

profile of v2, /device:TPU:1, one launch (start us, length us, event | category | flops | bytes accessed | tf_op | source)
XLA Modules:
  0.0 41.9 jit_solution(8173896197253018113)
XLA Ops:
  0.0 39.8 %shard_map.73 = bf16[32,24,512]{2,1,0:T(8,128)(2,1)} custom-call(s32[1,32]{1,0:T(1,128)} %bitcast.3, s32[8,8]{1,0:T(8,128)} %slots_in.1, bf16[32,24,512]{2,1,0:T(8,128)(2,1)} %tiles_in.1, bf16[8,96,192]{2,1,0:T(8,128)(2,1)} %down_in.1, f32[1,192]{1,0:T(1,128)} %bitcast.2, bf16[192,192]{1,0:T(8,128)(2,1)} %mid_in.1, bf16[8,192,96]{2,1,0:T(8,128)(2,1)} %up_in.1), custom_call_target="tpu_custom_call" | custom-call | tf_op jit(solution)/shard_map/pallas_call | solution.py:351
  39.8 2.1 %copy.9 = bf16[32,24,512]{2,1,0:T(8,128)(2,1)} copy(bf16[32,24,512]{2,1,0:T(8,128)(2,1)} %shard_map.73) | data formatting | bytes 1572864

commit v3 on v2

--- a/solution.py
+++ b/solution.py
@@ -137,7 +137,7 @@
 
     for p in range(pieces_in):
         loads[3 + p].wait()
-        lax.fori_loop(p * piece // 4, (p + 1) * piece // 4, down, 0)
+        lax.fori_loop(p * piece // 4, (p + 1) * piece // 4, down, 0, unroll=2)
 
     pl.semaphore_wait(barrier, n + 1)
 
@@ -179,6 +179,16 @@
 
     def joined(ref, ch, first, second):
         return jnp.where(left, ref[ch, first].astype(F32), ref[ch, second].astype(F32))
+
+    def mate(step):
+        off = n - step
+        if n & (n - 1):
+            return lax.rem(me + off, n)
+        d, bit = me, 1
+        while bit < n:
+            d = d + (off // bit) % 2 * (1 - 2 * ((me // bit) % 2)) * bit
+            bit *= 2
+        return d
 
     def exchange(src, dst, send, recv, ch, d):
         return to(src.at[ch, d], dst.at[ch, me], send.at[ch], recv.at[ch], d, rank)
@@ -205,14 +215,14 @@
         acts[ch, 2 * pairs] = silu(b).astype(BF16)
 
         def send(off, carry, ch=ch):
-            d = lax.rem(me + off, n)
+            d = mate(off)
             for m in range(per_dest):
                 t = d * capacity + 2 * m
                 going[ch, d, m] = joined(acts, ch, index[0, t], index[0, t + 1]).astype(BF16)
             exchange(going, arrived, go_s, go_r, ch, d).start()
             return carry
 
-        lax.fori_loop(1, n, send, 0)
+        lax.fori_loop(1, n, send, 0, unroll=n - 1 if n <= 8 else 1)
         for m in range(per_dest):
             t = me * capacity + 2 * m
             arrived[ch, me, m] = joined(acts, ch, index[0, t], index[0, t + 1]).astype(BF16)
@@ -257,41 +267,46 @@
             return sums
 
         def send_back(off, carry, ch=ch, paired=paired):
-            d = lax.rem(me + off, n)
+            d = mate(off)
             for m, value in enumerate(paired(d)):
                 back[ch, d, m] = value
             exchange(back, returned, back_s, back_r, ch, d).start()
             return carry
 
-        lax.fori_loop(1, n, send_back, 0)
+        lax.fori_loop(1, n, send_back, 0, unroll=n - 1 if n <= 8 else 1)
         for m, value in enumerate(paired(me)):
             returned[ch, me, m] = value
 
-    shares = [
-        to(full.at[lo, ch, hi], full.at[lo, ch, hi], share_s.at[ch], share_r.at[ch], me, x_peer)
-        for ch in range(chunks)
-    ]
-    alls = [
-        to(full.at[lo, ch], full.at[lo, ch], all_s.at[ch], all_r.at[ch], me, core_peer)
-        for ch in range(chunks)
-    ]
+    parts = 2
+    span = pairs // parts
+    shares, alls = [], []
+    for ch in range(chunks):
+        for p in range(parts):
+            at, sem = pl.ds(p * span, span), ch * parts + p
+            own = full.at[lo, ch, hi, at]
+            shares.append(to(own, own, share_s.at[sem], share_r.at[sem], me, x_peer))
+            both = full.at[lo, ch, :, at]
+            alls.append(to(both, both, all_s.at[sem], all_r.at[sem], me, core_peer))
+
+    def pass_on(ch):
+        for i in range(ch * parts, (ch + 1) * parts):
+            shares[i].wait_recv()
+            alls[i].start()
+
     for ch in range(chunks):
         whole(back, returned, back_s, back_r, ch).wait_recv()
-        spread(
-            again, ch, returned[ch].astype(F32).reshape(half * ROWS, LANES), half
-        )
+        spread(again, ch, returned[ch].astype(F32).reshape(half * ROWS, LANES), half)
 
         def collect(m, carry, ch=ch):
             full[lo, ch, hi, m] = joined(again, ch, index[2, 2 * m], index[2, 2 * m + 1]).astype(BF16)
             return carry
 
-        lax.fori_loop(0, pairs, collect, 0, unroll=4)
-        shares[ch].start()
-    for ch in range(chunks):
-        shares[ch].wait_recv()
-        alls[ch].start()
-    for ch in range(chunks):
-        alls[ch].wait_recv()
+        for p in range(parts):
+            lax.fori_loop(p * span, (p + 1) * span, collect, 0, unroll=8)
+            shares[ch * parts + p].start()
+        if ch > 0:
+            pass_on(ch - 1)
+    pass_on(chunks - 1)
 
     def up(step, carry):
         x = jnp.concatenate(
@@ -316,7 +331,10 @@
 
     stores = []
     for p in range(pieces_in):
-        lax.fori_loop(p * piece // 4, (p + 1) * piece // 4, up, 0)
+        if p % (pieces_in // parts) == 0:
+            for ch in range(chunks):
+                alls[ch * parts + p // (pieces_in // parts)].wait_recv()
+        lax.fori_loop(p * piece // 4, (p + 1) * piece // 4, up, 0, unroll=2)
         at = pl.ds(p * piece, piece)
         stores.append(pltpu.make_async_copy(tiles.at[at], out.at[at], store_s.at[p]))
         stores[p].start()
@@ -326,8 +344,8 @@
         xs[ch].wait_send()
         whole(going, arrived, go_s, go_r, ch).wait_send()
         whole(back, returned, back_s, back_r, ch).wait_send()
-        shares[ch].wait_send()
-        alls[ch].wait_send()
+    for copy in shares + alls:
+        copy.wait_send()
     for store in stores:
         store.wait()
 
@@ -383,7 +401,8 @@
             buffer(chunks, 2 * half),
             buffer(2, chunks, 2, pairs),
         ]
-        + [pltpu.SemaphoreType.DMA((chunks,))] * 12,
+        + [pltpu.SemaphoreType.DMA((chunks,))] * 8
+        + [pltpu.SemaphoreType.DMA((2 * chunks,))] * 4,
         compiler_params=pltpu.CompilerParams(
             collective_id=0, has_side_effects=True, vmem_limit_bytes=62 * 1024 * 1024
         ),

time: 42 us -> 38.9 us (0.926)
  Pallas kernels: 39.8 us -> 36.7 us
    pallas_call x1, Pallas kernels: 39.8 us -> 36.7 us  [local(): pl.pallas_call(functools.partial(main_kernel, n, capacity), out_shape=jax...]
where the time goes in v3:
time: 38.9 us; the launch traced here: 38.8 us
  Pallas kernels  36.7 us (94%)
  local copies, waits for them, and re-layouts  2.06 us (5%)
    pallas_call x1, Pallas kernels, local(): pl.pallas_call(functools.partial(main_kernel, n, capacity), out_shape=jax...  36.7 us
    unnamed x1, local copies, waits for them, and re-layouts  2.06 us

profile of v3, /device:TPU:1, one launch (start us, length us, event | category | flops | bytes accessed | tf_op | source)
XLA Modules:
  0.0 38.8 jit_solution(8127794818348470177)
XLA Ops:
  0.0 36.7 %shard_map.73 = bf16[32,24,512]{2,1,0:T(8,128)(2,1)} custom-call(s32[1,32]{1,0:T(1,128)} %bitcast.3, s32[8,8]{1,0:T(8,128)} %slots_in.1, bf16[32,24,512]{2,1,0:T(8,128)(2,1)} %tiles_in.1, bf16[8,96,192]{2,1,0:T(8,128)(2,1)} %down_in.1, f32[1,192]{1,0:T(1,128)} %bitcast.2, bf16[192,192]{1,0:T(8,128)(2,1)} %mid_in.1, bf16[8,192,96]{2,1,0:T(8,128)(2,1)} %up_in.1), custom_call_target="tpu_custom_call" | custom-call | tf_op jit(solution)/shard_map/pallas_call | solution.py:369
  36.7 2.1 %copy.9 = bf16[32,24,512]{2,1,0:T(8,128)(2,1)} copy(bf16[32,24,512]{2,1,0:T(8,128)(2,1)} %shard_map.73) | data formatting | bytes 1572864

commit v4 on v3

--- a/solution.py
+++ b/solution.py
@@ -51,7 +51,7 @@
     share_s, share_r, all_s, all_r,
 ):
     blocks, fine_share, voxels = tiles.shape
-    pieces_in = 4
+    pieces_in = 2
     piece = blocks // pieces_in
     sources = [(down_in, w_down), (route_in, route), (slots_in, slots)]
     for p in range(pieces_in):
@@ -137,7 +137,7 @@
 
     for p in range(pieces_in):
         loads[3 + p].wait()
-        lax.fori_loop(p * piece // 4, (p + 1) * piece // 4, down, 0, unroll=2)
+        lax.fori_loop(p * piece // 4, (p + 1) * piece // 4, down, 0, unroll=4)
 
     pl.semaphore_wait(barrier, n + 1)
 
@@ -179,16 +179,6 @@
 
     def joined(ref, ch, first, second):
         return jnp.where(left, ref[ch, first].astype(F32), ref[ch, second].astype(F32))
-
-    def mate(step):
-        off = n - step
-        if n & (n - 1):
-            return lax.rem(me + off, n)
-        d, bit = me, 1
-        while bit < n:
-            d = d + (off // bit) % 2 * (1 - 2 * ((me // bit) % 2)) * bit
-            bit *= 2
-        return d
 
     def exchange(src, dst, send, recv, ch, d):
         return to(src.at[ch, d], dst.at[ch, me], send.at[ch], recv.at[ch], d, rank)
@@ -215,7 +205,7 @@
         acts[ch, 2 * pairs] = silu(b).astype(BF16)
 
         def send(off, carry, ch=ch):
-            d = mate(off)
+            d = lax.rem(me + off, n)
             for m in range(per_dest):
                 t = d * capacity + 2 * m
                 going[ch, d, m] = joined(acts, ch, index[0, t], index[0, t + 1]).astype(BF16)
@@ -267,7 +257,7 @@
             return sums
 
         def send_back(off, carry, ch=ch, paired=paired):
-            d = mate(off)
+            d = lax.rem(me + off, n)
             for m, value in enumerate(paired(d)):
                 back[ch, d, m] = value
             exchange(back, returned, back_s, back_r, ch, d).start()
@@ -334,7 +324,7 @@
         if p % (pieces_in // parts) == 0:
             for ch in range(chunks):
                 alls[ch * parts + p // (pieces_in // parts)].wait_recv()
-        lax.fori_loop(p * piece // 4, (p + 1) * piece // 4, up, 0, unroll=2)
+        lax.fori_loop(p * piece // 4, (p + 1) * piece // 4, up, 0, unroll=4)
         at = pl.ds(p * piece, piece)
         stores.append(pltpu.make_async_copy(tiles.at[at], out.at[at], store_s.at[p]))
         stores[p].start()
@@ -381,8 +371,8 @@
             pltpu.VMEM(parent_slots.shape, jnp.int32),
             pltpu.VMEM((8, lanes), jnp.int32),
             pltpu.SMEM((8, lanes), jnp.int32),
-            pltpu.SemaphoreType.DMA((10,)),
-            pltpu.SemaphoreType.DMA((4,)),
+            pltpu.SemaphoreType.DMA((8,)),
+            pltpu.SemaphoreType.DMA((2,)),
             pltpu.SemaphoreType.DMA,
             pltpu.VMEM((2, width, LANES), BF16),
             pltpu.VMEM((width, width), BF16),

time: 38.9 us -> 38.2 us (0.982)
  Pallas kernels: 36.7 us -> 35.9 us
    pallas_call x1, Pallas kernels: 36.7 us -> 35.9 us  [local(): pl.pallas_call(functools.partial(main_kernel, n, capacity), out_shape=jax...]
where the time goes in v4:
time: 38.2 us; the launch traced here: 38 us
  Pallas kernels  35.9 us (94%)
  local copies, waits for them, and re-layouts  2.06 us (5%)
    pallas_call x1, Pallas kernels, local(): pl.pallas_call(functools.partial(main_kernel, n, capacity), out_shape=jax...  35.9 us
    unnamed x1, local copies, waits for them, and re-layouts  2.06 us

profile of v4, /device:TPU:1, one launch (start us, length us, event | category | flops | bytes accessed | tf_op | source)
XLA Modules:
  0.0 38.0 jit_solution(3402534132203748724)
XLA Ops:
  0.0 35.9 %shard_map.73 = bf16[32,24,512]{2,1,0:T(8,128)(2,1)} custom-call(s32[1,32]{1,0:T(1,128)} %bitcast.3, s32[8,8]{1,0:T(8,128)} %slots_in.1, bf16[32,24,512]{2,1,0:T(8,128)(2,1)} %tiles_in.1, bf16[8,96,192]{2,1,0:T(8,128)(2,1)} %down_in.1, f32[1,192]{1,0:T(1,128)} %bitcast.2, bf16[192,192]{1,0:T(8,128)(2,1)} %mid_in.1, bf16[8,192,96]{2,1,0:T(8,128)(2,1)} %up_in.1), custom_call_target="tpu_custom_call" | custom-call | tf_op jit(solution)/shard_map/pallas_call | solution.py:359
  35.9 2.1 %copy.9 = bf16[32,24,512]{2,1,0:T(8,128)(2,1)} copy(bf16[32,24,512]{2,1,0:T(8,128)(2,1)} %shard_map.73) | data formatting | bytes 1572864

commit v5 on v4

--- a/solution.py
+++ b/solution.py
@@ -135,24 +135,26 @@
                         part[l, ch, h, step * 2 + u] = both[at : at + ROWS]
         return carry
 
-    for p in range(pieces_in):
-        loads[3 + p].wait()
-        lax.fori_loop(p * piece // 4, (p + 1) * piece // 4, down, 0, unroll=4)
-
-    pl.semaphore_wait(barrier, n + 1)
-
     def to(src, dst, send, recv, space, chan):
         return pltpu.make_async_remote_copy(
             src_ref=src, dst_ref=dst, send_sem=send, recv_sem=recv,
             device_id=(space, chan), device_id_type=MESH,
         )
 
-    cores = [
-        to(part.at[1 - lo, ch], core_in.at[ch], core_s.at[ch], core_r.at[ch], me, core_peer)
-        for ch in range(chunks)
-    ]
-    for copy in cores:
-        copy.start()
+    cores = []
+    for p in range(pieces_in):
+        loads[3 + p].wait()
+        lax.fori_loop(p * piece // 4, (p + 1) * piece // 4, down, 0, unroll=4)
+        if p == 0:
+            pl.semaphore_wait(barrier, n + 1)
+        at = pl.ds(p * piece // 2, piece // 2)
+        for ch in range(chunks):
+            i = p * chunks + ch
+            cores.append(
+                to(part.at[1 - lo, ch, :, at], core_in.at[ch, :, at], core_s.at[i], core_r.at[i],
+                   me, core_peer)
+            )
+            cores[i].start()
 
     loads[3 + pieces_in].wait()
     bias_t[...] = jnp.broadcast_to(bias[...], (LANES, width)).T.reshape(
@@ -161,7 +163,8 @@
 
     xs = [to(x_out.at[ch], x_in.at[ch], x_s.at[ch], x_r.at[ch], me, x_peer) for ch in range(chunks)]
     for ch in range(chunks):
-        cores[ch].wait_recv()
+        for copy in cores[ch::chunks]:
+            copy.wait_recv()
         x_out[ch] = (
             part[lo, ch, 1 - hi].astype(F32) + core_in[ch, 1 - hi].astype(F32)
         ).astype(BF16)
@@ -330,7 +333,8 @@
         stores[p].start()
 
     for ch in range(chunks):
-        cores[ch].wait_send()
+        for copy in cores[ch::chunks]:
+            copy.wait_send()
         xs[ch].wait_send()
         whole(going, arrived, go_s, go_r, ch).wait_send()
         whole(back, returned, back_s, back_r, ch).wait_send()
@@ -391,7 +395,8 @@
             buffer(chunks, 2 * half),
             buffer(2, chunks, 2, pairs),
         ]
-        + [pltpu.SemaphoreType.DMA((chunks,))] * 8
+        + [pltpu.SemaphoreType.DMA((2 * chunks,))] * 2
+        + [pltpu.SemaphoreType.DMA((chunks,))] * 6
         + [pltpu.SemaphoreType.DMA((2 * chunks,))] * 4,
         compiler_params=pltpu.CompilerParams(
             collective_id=0, has_side_effects=True, vmem_limit_bytes=62 * 1024 * 1024

time: 38.2 us -> 38 us (level)
  no operation moved by 1% of the time
where the time goes in v5:
time: 38 us; the launch traced here: 37.8 us
  Pallas kernels  35.7 us (94%)
  local copies, waits for them, and re-layouts  2.06 us (5%)
    pallas_call x1, Pallas kernels, local(): pl.pallas_call(functools.partial(main_kernel, n, capacity), out_shape=jax...  35.7 us
    unnamed x1, local copies, waits for them, and re-layouts  2.06 us

profile of v5, /device:TPU:1, one launch (start us, length us, event | category | flops | bytes accessed | tf_op | source)
XLA Modules:
  0.0 37.8 jit_solution(17358075244699657756)
XLA Ops:
  0.0 35.7 %shard_map.73 = bf16[32,24,512]{2,1,0:T(8,128)(2,1)} custom-call(s32[1,32]{1,0:T(1,128)} %bitcast.3, s32[8,8]{1,0:T(8,128)} %slots_in.1, bf16[32,24,512]{2,1,0:T(8,128)(2,1)} %tiles_in.1, bf16[8,96,192]{2,1,0:T(8,128)(2,1)} %down_in.1, f32[1,192]{1,0:T(1,128)} %bitcast.2, bf16[192,192]{1,0:T(8,128)(2,1)} %mid_in.1, bf16[8,192,96]{2,1,0:T(8,128)(2,1)} %up_in.1), custom_call_target="tpu_custom_call" | custom-call | tf_op jit(solution)/shard_map/pallas_call | solution.py:363
  35.7 2.1 %copy.9 = bf16[32,24,512]{2,1,0:T(8,128)(2,1)} copy(bf16[32,24,512]{2,1,0:T(8,128)(2,1)} %shard_map.73) | data formatting | bytes 1572864
